TPU v7x, 32 devices: a whole 2x2x4 slice. The times are simulated.
32 devices in a mesh: ctx: 8 (over z, x), head: 4 (over y, core).
Axes of the slice: x: 2, y: 2, z: 4, core: 2. Of those that a mesh axis runs over, the one named last changes fastest.
Arguments:
- tokens: bfloat16 [2048, 256], P('ctx'), may hold values from -6 to 6
- in_gain: float32 [256], replicated, may hold values from 0.1 to 1.9
- w_uvqk: bfloat16 [256, 8, 128], P(None, 'head'), may hold values from -0.375 to 0.375
- w_out: bfloat16 [256, 256], P('head'), may hold values from -0.375 to 0.375
- grad_out: bfloat16 [2048, 256], P('ctx'), may hold values from -6 to 6
- lengths: int32 [3], replicated, may hold values from 1 to 1024, 2048 in all
- block_order: int32 [16], replicated, may hold values from 0 to 15, each once
Outputs:
- tokens_grad: bfloat16 [2048, 256], P('ctx')
- uvqk_grad: float32 [256, 8, 128], P('ctx', 'head')
- out_weight_grad: float32 [256, 256], P('head', 'ctx')
Inputs may be any that keep to these rules, and one draw needn't show every extreme that they name: User history lengths in loader order, summing to 2048; the longest is exactly 1024. `block_order`: a permutation of the 16 blocks.
All inputs are finite; a program needn't handle non-finite values.
Results may differ from a plain program's by a relative error of at most 0.0075.
Values may be sent and summed in bfloat16 or wider, within the bound.
A program may use at most 64 MiB of HBM per device.

v0:
```python
import math

import jax
import jax.numpy as jnp
from jax import lax
from jax.sharding import PartitionSpec as P


def keep_same(totals):
    return totals


def pair_terms(query_part, key_part, value_part, grad_part, live, score_scale):
    scores = jnp.einsum("qhd,khd->hqk", query_part, key_part, preferred_element_type=jnp.float32)
    sigmoid = jax.nn.sigmoid(scores)
    weights = (jax.nn.silu(scores) * score_scale * live).astype(jnp.bfloat16)
    weight_grad = jnp.einsum(
        "qhd,khd->hqk", grad_part, value_part, preferred_element_type=jnp.float32
    )
    score_grad = (
        weight_grad * sigmoid * (1.0 + scores * (1.0 - sigmoid)) * score_scale * live
    ).astype(jnp.bfloat16)
    return (weights, score_grad)


def body(tokens, in_gain, w_uvqk, w_out, grad_out, lengths, block_order):
    row_count = tokens.shape[0]
    total = row_count * lax.axis_size("ctx")
    heads_here = w_uvqk.shape[1]
    head_dim = w_uvqk.shape[2] // 4
    local_width = heads_here * head_dim
    full_width = local_width * lax.axis_size("head")
    block_size = total // block_order.shape[0]
    score_scale = 1.0 / (total // 2)
    all_rows = jnp.arange(total, dtype=jnp.int32)
    events = block_order[all_rows // block_size] * block_size + all_rows % block_size
    ends = jnp.cumsum(lengths)
    owners = jnp.sum((events[:, None] >= ends[None, :]).astype(jnp.int32), axis=1)
    first_row = lax.axis_index("ctx") * row_count
    my_events = lax.dynamic_slice_in_dim(events, first_row, row_count)
    my_owners = lax.dynamic_slice_in_dim(owners, first_row, row_count)
    float_in = tokens.astype(jnp.float32)
    row_mean = jnp.mean(float_in, axis=1, keepdims=True)
    centered = float_in - row_mean
    inv_std = lax.rsqrt(jnp.mean(centered * centered, axis=1, keepdims=True) + 1e-05)
    normed = centered * inv_std
    scaled_in = (normed * in_gain).astype(jnp.bfloat16)
    pre_act = jnp.einsum("td,dhc->thc", scaled_in, w_uvqk, preferred_element_type=jnp.float32)
    activ = jax.nn.silu(pre_act).astype(jnp.bfloat16)
    units = activ[..., :head_dim]
    values = activ[..., head_dim : 2 * head_dim]
    queries = activ[..., 2 * head_dim : 3 * head_dim]
    keys = activ[..., 3 * head_dim :]
    kv_local = jnp.concatenate(
        [keys.reshape(row_count, local_width), values.reshape(row_count, local_width)], axis=1
    )
    kv_all = lax.all_gather(kv_local, "ctx", axis=0, tiled=True)
    key_block = math.gcd(total, 2048)
    key_count = total // key_block

    def key_slice(index):
        begin = index * key_block
        block_rows = lax.dynamic_slice_in_dim(kv_all, begin, key_block, 0)
        key_part = block_rows[:, :local_width].reshape(key_block, heads_here, head_dim)
        value_part = block_rows[:, local_width:].reshape(key_block, heads_here, head_dim)
        ev_part = lax.dynamic_slice_in_dim(events, begin, key_block)
        ow_part = lax.dynamic_slice_in_dim(owners, begin, key_block)
        live = (
            (my_owners[:, None] == ow_part[None, :]) & (ev_part[None, :] <= my_events[:, None])
        ).astype(jnp.float32)
        return (key_part, value_part, live)

    def forward_step(index, attended):
        key_part, value_part, live = key_slice(index)

        def forward_compute(current):
            scores = jnp.einsum(
                "qhd,khd->hqk", queries, key_part, preferred_element_type=jnp.float32
            )
            weights = (jax.nn.silu(scores) * score_scale * live).astype(jnp.bfloat16)
            return current + jnp.einsum(
                "hqk,khd->qhd", weights, value_part, preferred_element_type=jnp.float32
            )

        return lax.cond(jnp.any(live > 0.0), forward_compute, keep_same, attended)

    zero_heads = jnp.zeros((row_count, heads_here, head_dim), jnp.float32)
    attended = lax.fori_loop(0, key_count, forward_step, zero_heads).reshape(row_count, local_width)
    total_sum, total_square = lax.psum(
        (jnp.sum(attended, axis=1), jnp.sum(attended * attended, axis=1)), "head"
    )
    attn_mean = total_sum[:, None] / full_width
    attn_var = total_square[:, None] / full_width - attn_mean * attn_mean
    attn_inv = lax.rsqrt(attn_var + 1e-05)
    attn_norm = (attended - attn_mean) * attn_inv
    units_flat = units.reshape(row_count, local_width).astype(jnp.float32)
    gated = (attn_norm * units_flat).astype(jnp.bfloat16)
    gated_grad = lax.dot_general(
        grad_out, w_out, (((1,), (1,)), ((), ())), preferred_element_type=jnp.float32
    )
    out_weight_grad = lax.dot_general(
        gated, grad_out, (((0,), (0,)), ((), ())), preferred_element_type=jnp.float32
    )
    units_grad = gated_grad * attn_norm
    norm_grad = gated_grad * units_flat
    grad_sum, grad_cross = lax.psum(
        (jnp.sum(norm_grad, axis=1), jnp.sum(norm_grad * attn_norm, axis=1)), "head"
    )
    attn_grad = (
        norm_grad - grad_sum[:, None] / full_width - attn_norm * grad_cross[:, None] / full_width
    ) * attn_inv
    attn_grad = attn_grad.astype(jnp.bfloat16).reshape(row_count, heads_here, head_dim)

    def backward_step(query_grad, index):
        key_part, value_part, live = key_slice(index)

        def backward_compute(current):
            weights, score_grad = pair_terms(
                queries, key_part, value_part, attn_grad, live, score_scale
            )
            updated = current + jnp.einsum(
                "hqk,khd->qhd", score_grad, key_part, preferred_element_type=jnp.float32
            )
            key_term = jnp.einsum(
                "hqk,qhd->khd", score_grad, queries, preferred_element_type=jnp.float32
            )
            value_term = jnp.einsum(
                "hqk,qhd->khd", weights, attn_grad, preferred_element_type=jnp.float32
            )
            return (
                updated,
                jnp.concatenate(
                    [
                        key_term.reshape(key_block, local_width),
                        value_term.reshape(key_block, local_width),
                    ],
                    axis=1,
                ),
            )

        def skipped(current):
            return (current, jnp.zeros((key_block, 2 * local_width), jnp.float32))

        return lax.cond(jnp.any(live > 0.0), backward_compute, skipped, query_grad)

    query_grad, key_terms = lax.scan(
        backward_step, zero_heads, jnp.arange(key_count, dtype=jnp.int32)
    )
    kv_grad = lax.psum_scatter(
        key_terms.reshape(total, 2 * local_width), "ctx", scatter_dimension=0, tiled=True
    )
    key_grad = kv_grad[:, :local_width].reshape(row_count, heads_here, head_dim)
    value_grad = kv_grad[:, local_width:].reshape(row_count, heads_here, head_dim)
    act_grad = jnp.concatenate(
        [units_grad.reshape(row_count, heads_here, head_dim), value_grad, query_grad, key_grad],
        axis=2,
    )
    sigmoid_pre = jax.nn.sigmoid(pre_act)
    pre_grad = (act_grad * sigmoid_pre * (1.0 + pre_act * (1.0 - sigmoid_pre))).astype(jnp.bfloat16)
    input_part = jnp.einsum("thc,dhc->td", pre_grad, w_uvqk, preferred_element_type=jnp.float32)
    input_grad = lax.psum(input_part, "head")
    proj_grad = jnp.einsum("td,thc->dhc", scaled_in, pre_grad, preferred_element_type=jnp.float32)
    uvqk_grad, wout_grad = (
        lax.psum_scatter(proj_grad, "ctx", scatter_dimension=0, tiled=True),
        lax.psum_scatter(out_weight_grad, "ctx", scatter_dimension=1, tiled=True),
    )
    scaled_grad = input_grad * in_gain
    tokens_grad = (
        grad_out.astype(jnp.float32)
        + (
            scaled_grad
            - jnp.mean(scaled_grad, axis=1, keepdims=True)
            - normed * jnp.mean(scaled_grad * normed, axis=1, keepdims=True)
        )
        * inv_std
    )
    return (tokens_grad.astype(jnp.bfloat16), uvqk_grad, wout_grad)


def solution(mesh):
    in_specs = (
        P("ctx", None),
        P(),
        P(None, "head", None),
        P("head", None),
        P("ctx", None),
        P(),
        P(),
    )
    out_specs = (P("ctx", None), P("ctx", "head", None), P("head", "ctx"))
    return jax.shard_map(body, mesh=mesh, in_specs=in_specs, out_specs=out_specs, check_vma=False)
```

profile of v0, /device:TPU:0, one launch (start us, length us, event | category | flops | bytes accessed | tf_op | source)
XLA Modules:
  0.0 320.1 jit_solution(10876296025656683165)
XLA Ops:
  7.2 0.0 copy-start
  7.2 0.0 reduce-scatter.4.cloned.1.call-start
  7.6 0.8 reduce-window.8
  8.4 1.0 convert_reduce_fusion
  9.5 1.1 fusion.18
  10.6 2.0 fusion.38
  12.5 4.3 %compare_select_fusion.1 = s32[2048,1]{0,1:T(1,128)S(1)} fusion(s32[]{:T(128)} %bitcast.16, s32[]{:T(128)} %bitcast.17, s32[]{:T(128)} %bitcast.18, s32[]{:T(128)} %bitcast.19, s32[]{:T(128)} %bitcast.20, s32[]{:T(128)} %bitcast.22, s32[]{:T(128)} %bitcast.21), kind=kLoop, calls=%fused_computation.61 | loop fusion | flops 47104 | bytes 8220 | tf_op jit(solution)/shard_map/gather | solution.py:36
  16.9 5.7 %fusion.27 = s32[2048]{0:T(1024)S(1)} fusion(pred[2048]{0:T(1024)(128)(4,1)S(1)} %compare_reduce_fusion.1, pred[2048]{0:T(1024)(128)(4,1)S(1)} %compare_reduce_fusion.2, pred[2048]{0:T(1024)(128)(4,1)S(1)} %compare_reduce_fusion.3, pred[2048]{0:T(1024)(128)(4,1)S(1)} %compare_reduce_fusion.4, pred[2048]{0:T(1024)(128)(4,1)S(1)} %compare_reduce_fusion.5, ...), kind=kLoop, calls=%fused_computation.73 | loop fusion | flops 34816 | bytes 34852 | tf_op jit(solution)/shard_map/add | solution.py:36
  22.6 0.1 dynamic_slice.22
  22.7 0.1 convert_reduce_fusion.1
  22.8 0.1 dynamic_slice.21
  22.9 1.0 copy.22
  23.9 1.2 fusion.32
  25.1 0.1 multiply_convert_fusion.4
  25.2 33.0 %all_gather.3 = bf16[2048,128]{0,1:T(8,128)(2,1)S(1)} all-gather(bf16[256,128]{0,1:T(8,128)(2,1)S(1)} %pad_maximum_fusion.1), channel_id=1, replica_groups=mesh['ctx'=8,'head'=4] {'ctx'}, dimensions={0}, use_global_device_ids=true | all-gather | bytes 589824 | tf_op jit(solution)/shard_map/all_gather | solution.py:57
  58.2 0.8 fusion.35
  59.0 1.2 and_convert_fusion
  60.8 0.0 copy-start.3
  60.8 5.2 %conditional.2 = (f32[256,2,32]{0,2,1:T(8,128)S(1)}) conditional(s32[]{:T(128)} %convert_element_type.57, f32[256,2,32]{0,2,1:T(8,128)S(1)} %broadcast_in_dim.19, (bf16[256,2,32]{0,2,1:T(8,128)(2,1)S(1)}, bf16[2048,2,32]{0,2,1:T(8,128)(2,1)}, f32[256,2048]{1,0:T(8,128)S(1)}, bf16[2048,2,32]{0,2,1:T(8,128)(2,1)S(1)}, f32[256,2,32]{0,2,1:T(8,128)S(1)}) %tuple.75), branch_computations={%region_5.6_spmd, %region_6.7_spmd} | conditional | flops 141049856 | bytes 6979592 | solution.py:85
  60.9 1.5 broadcast_multiply_fusion
  62.4 3.6 %fusion.2 = f32[256,2,32]{0,2,1:T(8,128)S(1)} fusion(f32[256,2,32]{0,2,1:T(8,128)S(1)} %get-tuple-element.60, bf16[2048,2,32]{0,2,1:T(8,128)(2,1)S(1)} %get-tuple-element.80, bf16[256,2,32]{0,2,1:T(8,128)(2,1)S(1)} %get-tuple-element.61, bf16[2048,2,32]{0,2,1:T(8,128)(2,1)} %get-tuple-element.78, f32[256,2048]{1,0:T(8,128)} %broadcast_multiply_fusion), kind=kOutput, calls=%fused_computation.3 | convolution fusion | flops 140525568 | bytes 2785280 | tf_op jit(solution)/shard_map/while/body/eval_jaxpr/cond/branch_1_fun/hqk,khd->qhd/dot_general | solution.py:81
  66.1 5.7 %all-reduce.1 = (f32[256]{0:T(256)S(1)}, f32[256]{0:T(256)S(1)}) all-reduce(f32[256]{0:T(256)S(1)} %get-tuple-element.118, f32[256]{0:T(256)S(1)} %get-tuple-element.117), channel_id=1, replica_groups=mesh['ctx'=8,'head'=4] {'head'}, use_global_device_ids=true, to_apply=%region_10.11 | all-reduce | flops 512 | bytes 4096 | tf_op jit(solution)/shard_map/psum | solution.py:89
  71.7 0.0 copy-done
  71.7 0.0 copy-done.3
  71.7 0.2 fusion.26
  72.0 6.6 %all-reduce = (f32[256]{0:T(256)S(1)}, f32[256]{0:T(256)S(1)}) all-reduce(f32[256]{0:T(256)S(1)} %get-tuple-element.116, f32[256]{0:T(256)S(1)} %get-tuple-element.115), channel_id=1, replica_groups=mesh['ctx'=8,'head'=4] {'head'}, use_global_device_ids=true, to_apply=%region_14.15 | all-reduce | flops 512 | bytes 4096 | tf_op jit(solution)/shard_map/psum | solution.py:106
  78.6 0.0 copy-start.1
  78.7 0.0 copy-start.4
  78.7 7.6 %conditional.3 = (f32[256,2,32]{0,2,1:T(8,128)S(1)}, f32[2048,128]{0,1:T(8,128)S(1)}) conditional(s32[]{:T(128)} %convert_element_type.57, f32[256,2,32]{0,2,1:T(8,128)S(1)} %broadcast_in_dim.19, (bf16[256,64]{0,1:T(8,128)(2,1)S(1)}, bf16[2048,2,32]{0,2,1:T(8,128)(2,1)S(1)}, bf16[256,2,32]{0,2,1:T(8,128)(2,1)S(1)}, ...), branch_computations={%region_15.16_spmd, %region_16.17_spmd} | conditional | flops 353124352 | bytes 31457296 | solution.py:144
  78.7 0.2 broadcast_multiply_fusion.1
  78.9 1.7 fusion.39
  80.5 1.4 fusion.4
  82.0 2.0 multiply_convert_fusion.2
  84.0 1.7 fusion.5
  85.7 0.5 fusion.40
  86.2 0.1 pad_maximum_fusion
  86.3 0.0 copy-start.2
  86.3 1.0 copy-done.2
  87.3 0.0 reduce-scatter.4.cloned.1.call-update
  87.3 0.0 all-reduce.4.cloned.1.call-start
  87.3 64.4 %reduce-scatter.4.cloned.1.call-done = f32[256,128]{0,1:T(8,128)} async-done(((f32[2048,128]{0,1:T(8,128)}), f32[256,128]{0,1:T(8,128)}) %reduce-scatter.4.cloned.1.call-update) | async-done | bytes 131088 | tf_op jit(solution)/shard_map/reduce_scatter | solution.py:149
  151.8 0.9 fusion.36
  152.7 0.1 fusion.20
  152.8 0.9 convolution_bitcast_fusion.1
  153.7 0.0 all-reduce.4.cloned.1.call-update
  153.7 0.0 reduce-scatter.6.cloned.1.call-start
  153.8 0.0 copy-done.1
  153.8 0.0 copy-done.4
  153.8 1.0 fusion.21
  154.9 0.0 reduce-scatter.6.cloned.1.call-update
  154.9 0.0 reduce-scatter.8.cloned.1.call-start
  154.9 0.9 fusion.41
  155.8 0.0 reduce-scatter.8.cloned.1.call-update
  155.8 29.4 %all-reduce.4.cloned.1.call-done = f32[256,256]{1,0:T(8,128)} async-done(((f32[256,256]{1,0:T(8,128)}), f32[256,256]{1,0:T(8,128)}) %all-reduce.4.cloned.1.call-update) | async-done | bytes 262160 | tf_op jit(solution)/shard_map/psum | solution.py:161
  185.2 1.2 multiply_reduce_fusion
  186.4 1.8 fusion.17
  188.2 61.7 %reduce-scatter.6.cloned.1.call-done = f32[32,2,128]{2,0,1:T(8,128)} async-done(((f32[256,2,128]{2,0,1:T(8,128)}), f32[32,2,128]{2,0,1:T(8,128)}) %reduce-scatter.6.cloned.1.call-update) | async-done | bytes 32784 | tf_op jit(solution)/shard_map/reduce_scatter | solution.py:164
  249.9 1.4 copy.27
  251.3 62.3 %reduce-scatter.8.cloned.1.call-done = f32[64,32]{0,1:T(8,128)} async-done(((f32[64,256]{0,1:T(8,128)}), f32[64,32]{0,1:T(8,128)}) %reduce-scatter.8.cloned.1.call-update) | async-done | bytes 8208 | tf_op jit(solution)/shard_map/reduce_scatter | solution.py:165
  (19 shorter events, 0.5 us)
Async XLA Ops:
  7.2 64.6 %copy-start = (bf16[64,256]{1,0:T(8,128)(2,1)S(1)}, bf16[64,256]{1,0:T(8,128)(2,1)}, u32[]{:S(2)}) copy-start(bf16[64,256]{1,0:T(8,128)(2,1)} %param.14) | copy-start | bytes 98308
  7.2 144.6 %reduce-scatter.4.cloned.1.call-start = ((), (), s32[]{:S(2)}) async-start(), calls=%async_computation.3 | async-start | bytes 1179648 | tf_op jit(solution)/shard_map/reduce_scatter | solution.py:149
  60.8 10.9 %copy-start.3 = (bf16[256,256]{1,0:T(8,128)(2,1)S(1)}, bf16[256,256]{1,0:T(8,128)(2,1)}, u32[]{:S(2)}) copy-start(bf16[256,256]{1,0:T(8,128)(2,1)} %param.15) | copy-start | bytes 393220
  78.6 75.1 %copy-start.1 = (bf16[256,256]{1,0:T(8,128)(2,1)S(1)}, bf16[256,256]{1,0:T(8,128)(2,1)}, u32[]{:S(2)}) copy-start(bf16[256,256]{1,0:T(8,128)(2,1)} %param.11) | copy-start | bytes 393220
  78.7 75.1 %copy-start.4 = (f32[256]{0:T(256)S(1)}, f32[256]{0:T(256)}, u32[]{:S(2)}) copy-start(f32[256]{0:T(256)} %param.12) | copy-start | bytes 3076
  86.3 1.0 copy-start.2
  87.3 97.9 %all-reduce.4.cloned.1.call-start = ((), (), s32[]{:S(2)}) async-start(), calls=%async_computation.4 | async-start | bytes 524288 | tf_op jit(solution)/shard_map/psum | solution.py:161
  153.7 96.1 %reduce-scatter.6.cloned.1.call-start = ((), (), s32[]{:S(2)}) async-start(), calls=%async_computation.5 | async-start | bytes 294912 | tf_op jit(solution)/shard_map/reduce_scatter | solution.py:164
  154.9 158.7 %reduce-scatter.8.cloned.1.call-start = ((), (), s32[]{:S(2)}) async-start(), calls=%async_computation.6 | async-start | bytes 147456 | tf_op jit(solution)/shard_map/reduce_scatter | solution.py:165
Sparse Core Ops, SparseCore 0:
  87.4 64.3 reduce-scatter.3
  154.2 30.9 all-reduce.3
  188.5 61.2 reduce-scatter.5
  253.6 59.8 reduce-scatter.7
where the time goes:
time: 321 us; the launch traced here: 320 us
  waiting for transfers between devices  218 us (68%)
  blocking collectives  45.3 us (14%)
  other arithmetic  19.7 us (6%)
  matrix products  15.2 us (5%)
  between operations  14.6 us (5%)
  local copies, waits for them, and re-layouts  7.21 us (2%)
    reduce_scatter x1, waiting for transfers between devices, body(): lax.psum_scatter(key_terms.reshape(total, 2 * local_width), 'ctx', scatte...  64.4 us
    reduce_scatter x1, waiting for transfers between devices, body(): lax.psum_scatter(out_weight_grad, 'ctx', scatter_dimension=1, tiled=True)  62.3 us
    reduce_scatter x1, waiting for transfers between devices, body(): lax.psum_scatter(proj_grad, 'ctx', scatter_dimension=0, tiled=True)  61.7 us
    all_gather x1, blocking collectives, body(): kv_all = lax.all_gather(kv_local, 'ctx', axis=0, tiled=True)  33 us
    psum x1, waiting for transfers between devices, body(): input_grad = lax.psum(input_part, 'head')  29.4 us
    psum x1, blocking collectives, body(): lax.psum((jnp.sum(norm_grad, axis=1), jnp.sum(norm_grad * attn_norm, axis...  6.64 us
  transfers between devices with their start and end apart: 4, of which 4 were waited for; matrix products, arithmetic and copies ran while one was open for 2% of the time, Pallas kernels for 0%

commit v1 on v0

v1 whole, which is shorter than its diff:
```python
import functools

import jax
import jax.numpy as jnp
from jax import lax
from jax.experimental import pallas as pl
from jax.experimental.pallas import tpu as pltpu
from jax.sharding import PartitionSpec as P

F32 = jnp.float32
BF16 = jnp.bfloat16
LANES = 128
MESH = pl.DeviceIdType.MESH


def dot_nt(a, b):
    return lax.dot_general(a, b, (((1,), (1,)), ((), ())), preferred_element_type=F32)


def dot_nn(a, b):
    return lax.dot_general(a, b, (((1,), (0,)), ((), ())), preferred_element_type=F32)


def dot_tn(a, b):
    return lax.dot_general(a, b, (((0,), (0,)), ((), ())), preferred_element_type=F32)


def silu_parts(scores, scale):
    sigma = 0.5 * jnp.tanh(0.5 * scores) + 0.5
    silu = scores * sigma
    return (silu * scale).astype(BF16), (sigma + silu * (1.0 - sigma)) * scale


def kernel(
    n, m, block, users, score_scale, keep,
    lengths_ref, order_ref, tokens_ref, gain_ref, w_ref, wout_ref, gout_ref,
    tok_ref, uvqk_ref, wo_ref,
    kv_all, q_all, ag_all, st_all, wo_send, wo_recv, uv_send, uv_recv,
    ip_send, ip_recv, tg_all, normed_ref, istd_ref, pre_ref, evq_ref, stq_ref,
    acc_ref, acck_ref, accv_ref, dq_ref, wk_ref, dk_ref,
    c_send, c_recv, h_send, h_recv,
):
    me = lax.axis_index("ctx")
    hd = lax.axis_index("head")
    rows, width = tokens_ref.shape
    half = rows // 2
    part = rows // m
    chunk = width // n

    barrier = pltpu.get_barrier_semaphore()

    def greet_ctx(s, c):
        pl.semaphore_signal(
            barrier, inc=1, device_id={"ctx": lax.rem(me + s, n)}, device_id_type=MESH
        )
        return c

    def greet_head(s, c):
        pl.semaphore_signal(
            barrier, inc=1, device_id={"head": lax.rem(hd + s, m)}, device_id_type=MESH
        )
        return c

    lax.fori_loop(1, n, greet_ctx, 0)
    lax.fori_loop(1, m, greet_head, 0)

    def ctx_copy(kind, src, dst, slot, sem, peer):
        return pltpu.make_async_remote_copy(
            src_ref=src.at[slot],
            dst_ref=dst.at[sem],
            send_sem=c_send.at[kind, slot if src is not dst else peer],
            recv_sem=c_recv.at[kind, sem],
            device_id={"ctx": peer},
            device_id_type=MESH,
        )

    def head_copy(kind, src, dst, slot, sem, peer):
        return pltpu.make_async_remote_copy(
            src_ref=src.at[slot],
            dst_ref=dst.at[sem],
            send_sem=h_send.at[kind, slot if src is not dst else peer],
            recv_sem=h_recv.at[kind, sem],
            device_id={"head": peer},
            device_id_type=MESH,
        )

    def spread(copy, kind, src, dst, mine, count, scatter):
        def step(s, c):
            peer = lax.rem(mine + s, count)
            copy(kind, src, dst, peer if scatter else mine, mine, peer).start()
            return c

        lax.fori_loop(1, count, step, 0)

    def arrived(copy, kind, src, dst, mine, count, scatter, s):
        origin = lax.rem(mine + count - s, count)
        copy(kind, src, dst, origin if scatter else mine, origin, origin).wait_recv()
        return origin

    def sent(copy, kind, src, dst, mine, count, scatter):
        def step(s, c):
            peer = lax.rem(mine + s, count)
            copy(kind, src, dst, peer if scatter else mine, mine, peer).wait_send()
            return c

        lax.fori_loop(1, count, step, 0)

    x = tokens_ref[...].astype(F32)
    centered = x - jnp.mean(x, axis=1, keepdims=True)
    istd = lax.rsqrt(jnp.mean(centered * centered, axis=1, keepdims=True) + 1e-05)
    normed = centered * istd
    normed_ref[...] = normed
    istd_ref[...] = jnp.broadcast_to(istd, (rows, LANES))
    scaled_in = (normed * gain_ref[...]).astype(BF16)
    pre = dot_nn(scaled_in, w_ref[...])
    pre_ref[...] = pre
    act = pre * (0.5 * jnp.tanh(0.5 * pre) + 0.5)
    act_a = act[:, :LANES].astype(BF16)
    act_b = act[:, LANES:].astype(BF16)
    kv_all[me] = act_b
    lane = lax.broadcasted_iota(jnp.int32, (rows, LANES), 1)
    low = lane < 64
    head0 = (lane & 32) == 0
    low_half = lax.broadcasted_iota(jnp.int32, (half, LANES), 1) < 64
    q_all[me] = jnp.where(
        low_half, pltpu.roll(act[:half, :LANES], 64, 1), act[half:, :LANES]
    ).astype(BF16)

    pl.semaphore_wait(barrier, n + m - 2)
    spread(ctx_copy, 0, kv_all, kv_all, me, n, False)
    spread(ctx_copy, 1, q_all, q_all, me, n, False)

    ends = []
    running = jnp.int32(0)
    for u in range(users):
        running = running + lengths_ref[u]
        ends.append(running)

    def starts(events):
        begin = jnp.zeros_like(events)
        for end in ends:
            begin = jnp.where(events >= end, end, begin)
        return begin

    row = lax.broadcasted_iota(jnp.int32, (rows, 2 * LANES), 0)
    ev_q = jnp.where(
        row < block, order_ref[2 * me] * block + row, (order_ref[2 * me + 1] - 1) * block + row
    )
    evq_ref[...] = ev_q
    stq_ref[...] = starts(ev_q)

    zero_a = jnp.zeros_like(act_a)
    picks_low = [low & head0, low & ~head0]
    picks_high = [(~low) & head0, (~low) & ~head0]
    rolled_b = pltpu.roll(act[:, LANES:], 64, 1).astype(BF16)

    def masked(values, picks):
        return [jnp.where(pick, values, zero_a) for pick in picks]

    q_heads = masked(act_a, picks_high)
    units = jnp.where(low, act_a, zero_a).astype(F32)
    gout = gout_ref[...]
    wout_wide = jnp.concatenate([wout_ref[...], jnp.zeros_like(wout_ref[...])], axis=0)
    gated_grad = dot_nt(gout, wout_wide)
    norm_grad = gated_grad * units

    acc_ref[...] = jnp.zeros_like(acc_ref)
    key_lane = lax.broadcasted_iota(jnp.int32, (1, 2 * LANES), 1)

    def query_live(p):
        ev_j = jnp.where(
            key_lane < block,
            order_ref[2 * p] * block + key_lane,
            (order_ref[2 * p + 1] - 1) * block + key_lane,
        )
        live = (ev_j <= evq_ref[...]) & (ev_j >= stq_ref[...])
        return jnp.where(live, score_scale, 0.0)

    def forward(s, c):
        @pl.when(s > 0)
        def _():
            arrived(ctx_copy, 0, kv_all, kv_all, me, n, False, s)

        p = lax.rem(me + n - s, n)
        kv = kv_all[p]
        scale = query_live(p)
        for h in range(2):
            weights, slope = silu_parts(dot_nt(q_heads[h], kv), scale)
            if keep:
                dq_ref[p, h] = slope
            acc_ref[h] += dot_nn(weights, kv)
        return c

    lax.fori_loop(0, n, forward, 0)
    attended = jnp.where(low, jnp.where(head0, acc_ref[0], acc_ref[1]), 0.0)

    def total(v):
        return jnp.sum(v, axis=1, keepdims=True)

    cols = jnp.where(lane == 0, total(attended), 0.0)
    cols = jnp.where(lane == 1, total(attended * attended), cols)
    cols = jnp.where(lane == 2, total(norm_grad), cols)
    cols = jnp.where(lane == 3, total(norm_grad * attended), cols)
    st_all[hd] = jnp.transpose(cols)[:8]
    spread(head_copy, 0, st_all, st_all, hd, m, False)

    lane_half = lax.broadcasted_iota(jnp.int32, (1, LANES), 1)
    ev_k = evq_ref[:, :LANES]
    k_heads = [masked(rolled_b, picks_low), masked(act_b, picks_high)]
    v_heads = [masked(act_b, picks_low), masked(rolled_b, picks_high)]

    def key_parts(p, part_no):
        ev_i = order_ref[2 * p + part_no] * block + lane_half
        live = (evq_ref[:, :LANES] <= ev_i) & (evq_ref[:, :LANES] >= starts(ev_i))
        scale = jnp.where(live, score_scale, 0.0)
        q = q_all[p]
        return [silu_parts(dot_nt(k_heads[part_no][h], q), scale) for h in range(2)]

    def key_prepare(s, c):
        @pl.when(s > 0)
        def _():
            arrived(ctx_copy, 1, q_all, q_all, me, n, False, s)

        if keep:
            p = lax.rem(me + n - s, n)
            for part_no in range(2):
                for h, (weights, slope) in enumerate(key_parts(p, part_no)):
                    wk_ref[p, part_no, h] = weights
                    dk_ref[p, part_no, h] = slope
        return c

    def stats_in(s, c):
        arrived(head_copy, 0, st_all, st_all, hd, m, False, s)
        return c

    lax.fori_loop(1, m, stats_in, 0)
    stats = st_all[0]
    for i in range(1, m):
        stats = stats + st_all[i]
    stats = jnp.transpose(jnp.concatenate([stats] * 16, axis=0)) / width
    attn_mean = stats[:, 0:1]
    attn_inv = lax.rsqrt(stats[:, 1:2] - attn_mean * attn_mean + 1e-05)
    grad_mean = stats[:, 2:3]
    cross_mean = (stats[:, 3:4] - attn_mean * grad_mean) * attn_inv
    attn_norm = jnp.where(low, (attended - attn_mean) * attn_inv, 0.0)
    attn_grad = jnp.where(low, (norm_grad - grad_mean - attn_norm * cross_mean) * attn_inv, 0.0)
    ag_all[me] = jnp.where(
        low_half, attn_grad[:half], pltpu.roll(attn_grad[half:], 64, 1)
    ).astype(BF16)
    spread(ctx_copy, 2, ag_all, ag_all, me, n, False)

    units_grad = gated_grad * attn_norm
    gated = (attn_norm * units).astype(BF16)
    wo_part = dot_tn(gout, gated).astype(BF16)
    if wo_send.shape[1] != chunk:
        wo_send[...] = jnp.zeros_like(wo_send)
        uv_send[...] = jnp.zeros_like(uv_send)
    for i in range(n):
        wo_send[i, :chunk] = wo_part[i * chunk : (i + 1) * chunk]
    spread(ctx_copy, 3, wo_send, wo_recv, me, n, True)

    attn_grad = attn_grad.astype(BF16)
    ag_heads = masked(attn_grad, picks_low)
    lax.fori_loop(0, n, key_prepare, 0)
    acc_ref[...] = jnp.zeros_like(acc_ref)

    def query_back(p, c):
        kv = kv_all[p]
        if not keep:
            scale = query_live(p)
        for h in range(2):
            if keep:
                slope = dq_ref[p, h]
            else:
                _, slope = silu_parts(dot_nt(q_heads[h], kv), scale)
            score_grad = (dot_nt(ag_heads[h], kv) * slope).astype(BF16)
            acc_ref[h] += dot_nn(score_grad, kv)
        return c

    lax.fori_loop(0, n, query_back, 0)
    query_grad = jnp.where(head0, acc_ref[0], acc_ref[1])

    acck_ref[...] = jnp.zeros_like(acck_ref)
    accv_ref[...] = jnp.zeros_like(accv_ref)

    def key_back(s, c):
        @pl.when(s > 0)
        def _():
            arrived(ctx_copy, 2, ag_all, ag_all, me, n, False, s)

        p = lax.rem(me + n - s, n)
        q = q_all[p]
        ag = ag_all[p]
        for part_no in range(2):
            parts = None if keep else key_parts(p, part_no)
            for h in range(2):
                if keep:
                    weights, slope = wk_ref[p, part_no, h], dk_ref[p, part_no, h]
                else:
                    weights, slope = parts[h]
                score_grad = (dot_nt(v_heads[part_no][h], ag) * slope).astype(BF16)
                acck_ref[part_no, h] += dot_nn(score_grad, q)
                accv_ref[part_no, h] += dot_nn(weights, ag)
        return c

    lax.fori_loop(0, n, key_back, 0)

    def fold(acc, part_no):
        return jnp.where(head0, acc[part_no, 0], acc[part_no, 1])

    key_grad = pltpu.roll(fold(acck_ref, 0), 64, 1) + fold(acck_ref, 1)
    value_grad = fold(accv_ref, 0) + pltpu.roll(fold(accv_ref, 1), 64, 1)
    act_grad = jnp.concatenate(
        [jnp.where(low, units_grad, query_grad), jnp.where(low, value_grad, key_grad)], axis=1
    )
    pre = pre_ref[...]
    sig = 0.5 * jnp.tanh(0.5 * pre) + 0.5
    pre_grad = (act_grad * (sig * (1.0 + pre * (1.0 - sig)))).astype(BF16)
    input_part = dot_nt(pre_grad, w_ref[...]).astype(BF16)
    for i in range(m):
        ip_send[i] = input_part[i * part : (i + 1) * part]
    spread(head_copy, 1, ip_send, ip_recv, hd, m, True)

    scaled_in = (normed_ref[...] * gain_ref[...]).astype(BF16)
    uv_part = dot_tn(scaled_in, pre_grad).astype(BF16)
    for i in range(n):
        uv_send[i, :chunk] = uv_part[i * chunk : (i + 1) * chunk]
    spread(ctx_copy, 4, uv_send, uv_recv, me, n, True)

    def parts_in(s, summed):
        origin = arrived(head_copy, 1, ip_send, ip_recv, hd, m, True, s)
        return summed + ip_recv[origin].astype(F32)

    input_grad = lax.fori_loop(1, m, parts_in, ip_send[hd].astype(F32))
    mine = pl.ds(pl.multiple_of(hd * part, part), part)
    scaled_grad = input_grad * gain_ref[...]
    my_normed = normed_ref[mine]
    my_istd = istd_ref[mine][:, 0:1]
    mean_a = jnp.mean(scaled_grad, axis=1, keepdims=True)
    mean_b = jnp.mean(scaled_grad * my_normed, axis=1, keepdims=True)
    tg_all[hd] = (
        gout_ref[mine].astype(F32) + (scaled_grad - mean_a - my_normed * mean_b) * my_istd
    ).astype(BF16)
    spread(head_copy, 2, tg_all, tg_all, hd, m, False)

    def wo_in(s, summed):
        origin = arrived(ctx_copy, 3, wo_send, wo_recv, me, n, True, s)
        return summed + wo_recv[origin].astype(F32)

    wo_sum = lax.fori_loop(1, n, wo_in, wo_send[me].astype(F32))
    wo_ref[...] = wo_sum[:chunk]

    def uv_in(s, summed):
        origin = arrived(ctx_copy, 4, uv_send, uv_recv, me, n, True, s)
        return summed + uv_recv[origin].astype(F32)

    uv_sum = lax.fori_loop(1, n, uv_in, uv_send[me].astype(F32))
    uvqk_ref[...] = uv_sum[:chunk]

    def tokens_in(s, c):
        arrived(head_copy, 2, tg_all, tg_all, hd, m, False, s)
        return c

    lax.fori_loop(1, m, tokens_in, 0)
    for i in range(m):
        tok_ref[i * part : (i + 1) * part] = tg_all[i]

    sent(ctx_copy, 0, kv_all, kv_all, me, n, False)
    sent(ctx_copy, 1, q_all, q_all, me, n, False)
    sent(ctx_copy, 2, ag_all, ag_all, me, n, False)
    sent(ctx_copy, 3, wo_send, wo_recv, me, n, True)
    sent(ctx_copy, 4, uv_send, uv_recv, me, n, True)
    sent(head_copy, 0, st_all, st_all, hd, m, False)
    sent(head_copy, 1, ip_send, ip_recv, hd, m, True)
    sent(head_copy, 2, tg_all, tg_all, hd, m, False)


def body(tokens, in_gain, w_uvqk, w_out, grad_out, lengths, block_order):
    rows, width = tokens.shape
    n = lax.axis_size("ctx")
    m = lax.axis_size("head")
    heads_here = w_uvqk.shape[1]
    head_dim = w_uvqk.shape[2] // 4
    total = rows * n
    block = total // block_order.shape[0]
    chunk = width // n
    padded = max(chunk, 16)
    keep = n <= 16
    kept = n if keep else 1
    w_cols = (
        w_uvqk.reshape(width, heads_here, 2, 2, head_dim)
        .transpose(0, 3, 2, 1, 4)
        .reshape(width, width)
    )
    vmem = pl.BlockSpec(memory_space=pltpu.VMEM)
    smem = pl.BlockSpec(memory_space=pltpu.SMEM)
    tok, uv, wo = pl.pallas_call(
        functools.partial(
            kernel, n, m, block, lengths.shape[0], 1.0 / (total // 2), keep
        ),
        out_shape=(
            jax.ShapeDtypeStruct((rows, width), BF16),
            jax.ShapeDtypeStruct((chunk, width), F32),
            jax.ShapeDtypeStruct((chunk, LANES), F32),
        ),
        in_specs=[smem, smem] + [vmem] * 5,
        out_specs=(vmem, vmem, vmem),
        scratch_shapes=[
            pltpu.VMEM((n, rows, LANES), BF16),
            pltpu.VMEM((n, rows // 2, LANES), BF16),
            pltpu.VMEM((n, rows // 2, LANES), BF16),
            pltpu.VMEM((m, 8, rows), F32),
            pltpu.VMEM((n, padded, LANES), BF16),
            pltpu.VMEM((n, padded, LANES), BF16),
            pltpu.VMEM((n, padded, width), BF16),
            pltpu.VMEM((n, padded, width), BF16),
            pltpu.VMEM((m, rows // m, width), BF16),
            pltpu.VMEM((m, rows // m, width), BF16),
            pltpu.VMEM((m, rows // m, width), BF16),
            pltpu.VMEM((rows, width), F32),
            pltpu.VMEM((rows, LANES), F32),
            pltpu.VMEM((rows, width), F32),
            pltpu.VMEM((rows, 2 * LANES), jnp.int32),
            pltpu.VMEM((rows, 2 * LANES), jnp.int32),
            pltpu.VMEM((2, rows, LANES), F32),
            pltpu.VMEM((2, 2, rows, LANES), F32),
            pltpu.VMEM((2, 2, rows, LANES), F32),
            pltpu.VMEM((kept, 2, rows, 2 * LANES), F32),
            pltpu.VMEM((kept, 2, 2, rows, LANES), BF16),
            pltpu.VMEM((kept, 2, 2, rows, LANES), F32),
            pltpu.SemaphoreType.DMA((5, n)),
            pltpu.SemaphoreType.DMA((5, n)),
            pltpu.SemaphoreType.DMA((3, m)),
            pltpu.SemaphoreType.DMA((3, m)),
        ],
        compiler_params=pltpu.CompilerParams(
            collective_id=0, has_side_effects=True, vmem_limit_bytes=40 * 1024 * 1024
        ),
    )(lengths, block_order, tokens, in_gain.reshape(1, width), w_cols, w_out, grad_out)
    uvqk_grad = (
        uv.reshape(chunk, 2, 2, heads_here, head_dim)
        .transpose(0, 3, 2, 1, 4)
        .reshape(chunk, heads_here, 4 * head_dim)
    )
    return tok, uvqk_grad, wo[:, : heads_here * head_dim].T


def solution(mesh):
    in_specs = (
        P("ctx", None),
        P(),
        P(None, "head", None),
        P("head", None),
        P("ctx", None),
        P(),
        P(),
    )
    out_specs = (P("ctx", None), P("ctx", "head", None), P("head", "ctx"))
    return jax.shard_map(body, mesh=mesh, in_specs=in_specs, out_specs=out_specs, check_vma=False)
```

time: 321 us -> 54 us (0.17)
  waiting for transfers between devices: 218 us -> 0 us
  Pallas kernels: 0 us -> 48.9 us
  blocking collectives: 45.3 us -> 0 us
  other arithmetic: 19.7 us -> 0 us
  matrix products: 15.2 us -> 0 us
  between operations: 14.6 us -> 0.73 us
    reduce_scatter x3 -> x0, waiting for transfers between devices: 188 us -> none  [the longest x1 64.4 us: body(): lax.psum_scatter(key_terms.reshape(total, 2 * local_width), 'ctx', scatte...]
    pallas_call x0 -> x1, Pallas kernels: none -> 48.9 us  [body(): pl.pallas_call(functools.partial(kernel, n, m, block, lengths.shape[0], 1...]
    all_gather x1 -> x0, blocking collectives: 33 us -> none  [body(): kv_all = lax.all_gather(kv_local, 'ctx', axis=0, tiled=True)]
    psum x1 -> x0, waiting for transfers between devices: 29.4 us -> none  [body(): input_grad = lax.psum(input_part, 'head')]
    dot_general x10 -> x0, matrix products: 14 us -> none  [the longest x1 3.64 us: forward_compute(): jnp.einsum('hqk,khd->qhd', weights, value_part, preferred_element_type=jn...]
    psum x2 -> x0, blocking collectives: 12.3 us -> none  [the longest x1 6.64 us: body(): lax.psum((jnp.sum(norm_grad, axis=1), jnp.sum(norm_grad * attn_norm, axis...]
    add x1 -> x0, other arithmetic: 5.72 us -> none  [body(): block_order[all_rows // block_size] * block_size + all_rows % block_size]
    gather x10 -> x0, other arithmetic: 4.73 us -> none  [body(): block_order[all_rows // block_size] * block_size + all_rows % block_size]
  transfers between devices with their start and end apart: 4 -> 0, of which waited for: 4 -> 0; matrix products, arithmetic and copies ran while one was open for 2% -> 0% of each run, Pallas kernels for 0% -> 0%
where the time goes in v1:
time: 54 us; the launch traced here: 53.8 us
  Pallas kernels  48.9 us (91%)
  local copies, waits for them, and re-layouts  4.24 us (8%)
  between operations  0.73 us (1%)
    pallas_call x1, Pallas kernels, body(): pl.pallas_call(functools.partial(kernel, n, m, block, lengths.shape[0], 1...  48.9 us
    unnamed x14, local copies, waits for them, and re-layouts  2.54 us

profile of v1, /device:TPU:0, one launch (start us, length us, event | category | flops | bytes accessed | tf_op | source)
XLA Modules:
  0.0 53.8 jit_solution(15333251806555167756)
XLA Ops:
  0.6 1.0 %copy.12 = bf16[256,2,128]{0,2,1:T(8,128)(2,1)S(1)} copy(bf16[256,2,128]{2,1,0:T(2,128)(2,1)} %param.9) | data formatting | bytes 262144 | tf_op args[2]
  1.7 0.0 copy-start.2
  1.7 0.0 copy-start.3
  1.7 0.0 copy-start.4
  1.7 0.0 copy-start.5
  1.7 0.0 copy-start
  1.7 0.0 copy-start.1
  1.7 0.1 copy.14.w_ref
  1.8 0.6 %copy-done.2 = bf16[64,256]{1,0:T(8,128)(2,1)S(1)} copy-done((bf16[64,256]{1,0:T(8,128)(2,1)S(1)}, bf16[64,256]{1,0:T(8,128)(2,1)}, u32[]{:S(2)}) %copy-start.2) | copy-done | bytes 32792
  2.4 0.0 copy-done.3
  2.4 0.0 copy-done.4
  2.4 0.0 copy-done.5
  2.4 0.2 copy-done
  2.6 0.1 copy-done.1
  2.7 48.9 %shard_map.94 = (bf16[256,256]{1,0:T(8,128)(2,1)S(1)}, f32[32,256]{1,0:T(8,128)S(1)}, f32[32,128]{1,0:T(8,128)S(1)}) custom-call(s32[3]{0:T(128)S(1)} %copy-done.4, s32[16]{0:T(128)S(1)} %copy-done.5, bf16[256,256]{1,0:T(8,128)(2,1)S(1)} %copy-done, f32[1,256]{1,0:T(1,128)S(1)} %bitcast.8, bf16[256,256]{1,0:T(8,128)(2,1)S(1)} %copy.14.w_ref, ...), custom_call_target="tpu_custom_call" | custom-call | tf_op jit(solution)/shard_map/pallas_call | solution.py:397
  51.6 0.6 %slice_bitcast_fusion = f32[64,32]{0,1:T(8,128)} fusion(f32[32,128]{1,0:T(8,128)S(1)} %get-tuple-element.8), kind=kLoop, calls=%fused_computation | loop fusion | bytes 16384 | tf_op jit(solution)/shard_map/transpose | solution.py:445
  52.2 0.1 reshape.24
  52.3 0.1 copy.15
  52.4 0.8 %reshape.25 = f32[32,2,128]{2,1,0:T(2,128)} reshape(f32[32,2,2,2,32]{4,3,2,1,0:T(2,128)S(1)} %copy.15) | data formatting | bytes 65536 | tf_op jit(solution)/shard_map/reshape | solution.py:443
  53.2 0.7 %copy.17 = bf16[256,256]{1,0:T(8,128)(2,1)} copy(bf16[256,256]{1,0:T(8,128)(2,1)S(1)} %get-tuple-element.12) | data formatting | bytes 262144
  (1 shorter events, 0.0 us)
Async XLA Ops:
  1.7 0.8 %copy-start.2 = (bf16[64,256]{1,0:T(8,128)(2,1)S(1)}, bf16[64,256]{1,0:T(8,128)(2,1)}, u32[]{:S(2)}) copy-start(bf16[64,256]{1,0:T(8,128)(2,1)} %wout_ref.1) | copy-start | bytes 98308
  1.7 0.8 %copy-start.3 = (f32[256]{0:T(256)S(1)}, f32[256]{0:T(256)}, u32[]{:S(2)}) copy-start(f32[256]{0:T(256)} %param.8) | copy-start | bytes 3076
  1.7 0.7 %copy-start.4 = (s32[3]{0:T(128)S(1)}, s32[3]{0:T(128)}, u32[]{:S(2)}) copy-start(s32[3]{0:T(128)} %lengths_ref.1) | copy-start | bytes 40
  1.7 0.7 %copy-start.5 = (s32[16]{0:T(128)S(1)}, s32[16]{0:T(128)}, u32[]{:S(2)}) copy-start(s32[16]{0:T(128)} %order_ref.1) | copy-start | bytes 196
  1.7 0.9 %copy-start = (bf16[256,256]{1,0:T(8,128)(2,1)S(1)}, bf16[256,256]{1,0:T(8,128)(2,1)}, u32[]{:S(2)}) copy-start(bf16[256,256]{1,0:T(8,128)(2,1)} %tokens_ref.1) | copy-start | bytes 393220
  1.7 1.0 %copy-start.1 = (bf16[256,256]{1,0:T(8,128)(2,1)S(1)}, bf16[256,256]{1,0:T(8,128)(2,1)}, u32[]{:S(2)}) copy-start(bf16[256,256]{1,0:T(8,128)(2,1)} %gout_ref.1) | copy-start | bytes 393220

commit v2 on v1

--- a/solution.py
+++ b/solution.py
@@ -97,6 +97,43 @@
         copy(kind, src, dst, origin if scatter else mine, origin, origin).wait_recv()
         return origin
 
+    lines = n // 2
+    pair = me + 1 - 2 * lax.rem(me, 2)
+
+    def line_origin(s):
+        return lax.rem(me + n - 2 * s, n)
+
+    def pair_origin(s):
+        return lax.rem(pair + n - 2 * s, n)
+
+    def hop(kind, buf, slot, sem, peer):
+        return pltpu.make_async_remote_copy(
+            src_ref=buf.at[slot],
+            dst_ref=buf.at[slot],
+            send_sem=c_send.at[kind, sem],
+            recv_sem=c_recv.at[kind, slot],
+            device_id={"ctx": peer},
+            device_id_type=MESH,
+        )
+
+    def gather(kind, buf):
+        def step(s, c):
+            peer = lax.rem(me + 2 * s, n)
+            hop(kind, buf, me, peer, peer).start()
+            return c
+
+        hop(kind, buf, me, pair, pair).start()
+        lax.fori_loop(1, lines, step, 0)
+
+    def relay(kind, buf, s):
+        origin = line_origin(s)
+        hop(kind, buf, origin, pair_origin(s), pair).wait_recv()
+        hop(kind, buf, origin, origin + 1 - 2 * lax.rem(origin, 2), pair).start()
+
+    def relayed(kind, buf, s):
+        origin = pair_origin(s)
+        hop(kind, buf, origin, origin, pair).wait_recv()
+
     def sent(copy, kind, src, dst, mine, count, scatter):
         def step(s, c):
             peer = lax.rem(mine + s, count)
@@ -112,23 +149,28 @@
     normed_ref[...] = normed
     istd_ref[...] = jnp.broadcast_to(istd, (rows, LANES))
     scaled_in = (normed * gain_ref[...]).astype(BF16)
-    pre = dot_nn(scaled_in, w_ref[...])
-    pre_ref[...] = pre
-    act = pre * (0.5 * jnp.tanh(0.5 * pre) + 0.5)
-    act_a = act[:, :LANES].astype(BF16)
-    act_b = act[:, LANES:].astype(BF16)
+
+    def project(cols):
+        pre = dot_nn(scaled_in, w_ref[:, cols])
+        pre_ref[:, cols] = pre
+        return pre * (0.5 * jnp.tanh(0.5 * pre) + 0.5)
+
+    wide_b = project(slice(LANES, 2 * LANES))
+    act_b = wide_b.astype(BF16)
     kv_all[me] = act_b
+    pl.semaphore_wait(barrier, n + m - 2)
+    gather(0, kv_all)
+    wide_a = project(slice(0, LANES))
+    act_a = wide_a.astype(BF16)
     lane = lax.broadcasted_iota(jnp.int32, (rows, LANES), 1)
     low = lane < 64
     head0 = (lane & 32) == 0
     low_half = lax.broadcasted_iota(jnp.int32, (half, LANES), 1) < 64
     q_all[me] = jnp.where(
-        low_half, pltpu.roll(act[:half, :LANES], 64, 1), act[half:, :LANES]
+        low_half, pltpu.roll(wide_a[:half], 64, 1), wide_a[half:]
     ).astype(BF16)
 
-    pl.semaphore_wait(barrier, n + m - 2)
-    spread(ctx_copy, 0, kv_all, kv_all, me, n, False)
-    spread(ctx_copy, 1, q_all, q_all, me, n, False)
+    gather(1, q_all)
 
     ends = []
     running = jnp.int32(0)
@@ -152,7 +194,7 @@
     zero_a = jnp.zeros_like(act_a)
     picks_low = [low & head0, low & ~head0]
     picks_high = [(~low) & head0, (~low) & ~head0]
-    rolled_b = pltpu.roll(act[:, LANES:], 64, 1).astype(BF16)
+    rolled_b = pltpu.roll(wide_b, 64, 1).astype(BF16)
 
     def masked(values, picks):
         return [jnp.where(pick, values, zero_a) for pick in picks]
@@ -176,12 +218,7 @@
         live = (ev_j <= evq_ref[...]) & (ev_j >= stq_ref[...])
         return jnp.where(live, score_scale, 0.0)
 
-    def forward(s, c):
-        @pl.when(s > 0)
-        def _():
-            arrived(ctx_copy, 0, kv_all, kv_all, me, n, False, s)
-
-        p = lax.rem(me + n - s, n)
+    def forward(p):
         kv = kv_all[p]
         scale = query_live(p)
         for h in range(2):
@@ -189,9 +226,24 @@
             if keep:
                 dq_ref[p, h] = slope
             acc_ref[h] += dot_nn(weights, kv)
-        return c
-
-    lax.fori_loop(0, n, forward, 0)
+
+    def forward_step(s, c):
+        @pl.when(s < lines)
+        def _():
+            @pl.when(s > 0)
+            def _():
+                relay(0, kv_all, s)
+
+            forward(line_origin(s))
+
+        @pl.when(s > 0)
+        def _():
+            relayed(0, kv_all, s - 1)
+            forward(pair_origin(s - 1))
+
+        return c
+
+    lax.fori_loop(0, lines + 1, forward_step, 0)
     attended = jnp.where(low, jnp.where(head0, acc_ref[0], acc_ref[1]), 0.0)
 
     def total(v):
@@ -216,18 +268,28 @@
         q = q_all[p]
         return [silu_parts(dot_nt(k_heads[part_no][h], q), scale) for h in range(2)]
 
-    def key_prepare(s, c):
-        @pl.when(s > 0)
-        def _():
-            arrived(ctx_copy, 1, q_all, q_all, me, n, False, s)
-
+    def key_prepare(p):
         if keep:
-            p = lax.rem(me + n - s, n)
             for part_no in range(2):
                 for h, (weights, slope) in enumerate(key_parts(p, part_no)):
                     wk_ref[p, part_no, h] = weights
                     dk_ref[p, part_no, h] = slope
-        return c
+
+    def relay_queries(s, c):
+        relay(1, q_all, s)
+        return c
+
+    def prepare_line(s, c):
+        key_prepare(line_origin(s))
+        return c
+
+    def prepare_pair(s, c):
+        relayed(1, q_all, s)
+        key_prepare(pair_origin(s))
+        return c
+
+    lax.fori_loop(1, lines, relay_queries, 0)
+    lax.fori_loop(0, lines, prepare_line, 0)
 
     def stats_in(s, c):
         arrived(head_copy, 0, st_all, st_all, hd, m, False, s)
@@ -247,7 +309,7 @@
     ag_all[me] = jnp.where(
         low_half, attn_grad[:half], pltpu.roll(attn_grad[half:], 64, 1)
     ).astype(BF16)
-    spread(ctx_copy, 2, ag_all, ag_all, me, n, False)
+    gather(2, ag_all)
 
     units_grad = gated_grad * attn_norm
     gated = (attn_norm * units).astype(BF16)
@@ -261,7 +323,13 @@
 
     attn_grad = attn_grad.astype(BF16)
     ag_heads = masked(attn_grad, picks_low)
-    lax.fori_loop(0, n, key_prepare, 0)
+    lax.fori_loop(0, lines, prepare_pair, 0)
+
+    def relay_grads(s, c):
+        relay(2, ag_all, s)
+        return c
+
+    lax.fori_loop(1, lines, relay_grads, 0)
     acc_ref[...] = jnp.zeros_like(acc_ref)
 
     def query_back(p, c):
@@ -283,12 +351,7 @@
     acck_ref[...] = jnp.zeros_like(acck_ref)
     accv_ref[...] = jnp.zeros_like(accv_ref)
 
-    def key_back(s, c):
-        @pl.when(s > 0)
-        def _():
-            arrived(ctx_copy, 2, ag_all, ag_all, me, n, False, s)
-
-        p = lax.rem(me + n - s, n)
+    def key_back(p):
         q = q_all[p]
         ag = ag_all[p]
         for part_no in range(2):
@@ -301,9 +364,18 @@
                 score_grad = (dot_nt(v_heads[part_no][h], ag) * slope).astype(BF16)
                 acck_ref[part_no, h] += dot_nn(score_grad, q)
                 accv_ref[part_no, h] += dot_nn(weights, ag)
-        return c
-
-    lax.fori_loop(0, n, key_back, 0)
+
+    def line_back(s, c):
+        key_back(line_origin(s))
+        return c
+
+    def pair_back(s, c):
+        relayed(2, ag_all, s)
+        key_back(pair_origin(s))
+        return c
+
+    lax.fori_loop(0, lines, line_back, 0)
+    lax.fori_loop(0, lines, pair_back, 0)
 
     def fold(acc, part_no):
         return jnp.where(head0, acc[part_no, 0], acc[part_no, 1])

time: 54 us -> 51.3 us (0.950)
  Pallas kernels: 48.9 us -> 46.2 us
    pallas_call x1, Pallas kernels: 48.9 us -> 46.2 us  [body(): pl.pallas_call(functools.partial(kernel, n, m, block, lengths.shape[0], 1...]
where the time goes in v2:
time: 51.3 us; the launch traced here: 51.2 us
  Pallas kernels  46.2 us (90%)
  local copies, waits for them, and re-layouts  4.24 us (8%)
  between operations  0.73 us (1%)
    pallas_call x1, Pallas kernels, body(): pl.pallas_call(functools.partial(kernel, n, m, block, lengths.shape[0], 1...  46.2 us
    unnamed x14, local copies, waits for them, and re-layouts  2.54 us

profile of v2, /device:TPU:0, one launch (start us, length us, event | category | flops | bytes accessed | tf_op | source)
XLA Modules:
  0.0 51.2 jit_solution(2125509916777080442)
XLA Ops:
  0.6 1.0 %copy.12 = bf16[256,2,128]{0,2,1:T(8,128)(2,1)S(1)} copy(bf16[256,2,128]{2,1,0:T(2,128)(2,1)} %param.9) | data formatting | bytes 262144 | tf_op args[2]
  1.7 0.0 copy-start.2
  1.7 0.0 copy-start.3
  1.7 0.0 copy-start.4
  1.7 0.0 copy-start.5
  1.7 0.0 copy-start
  1.7 0.0 copy-start.1
  1.7 0.1 copy.14.w_ref
  1.8 0.6 %copy-done.2 = bf16[64,256]{1,0:T(8,128)(2,1)S(1)} copy-done((bf16[64,256]{1,0:T(8,128)(2,1)S(1)}, bf16[64,256]{1,0:T(8,128)(2,1)}, u32[]{:S(2)}) %copy-start.2) | copy-done | bytes 32792
  2.4 0.0 copy-done.3
  2.4 0.0 copy-done.4
  2.4 0.0 copy-done.5
  2.4 0.2 copy-done
  2.6 0.1 copy-done.1
  2.7 46.2 %shard_map.94 = (bf16[256,256]{1,0:T(8,128)(2,1)S(1)}, f32[32,256]{1,0:T(8,128)S(1)}, f32[32,128]{1,0:T(8,128)S(1)}) custom-call(s32[3]{0:T(128)S(1)} %copy-done.4, s32[16]{0:T(128)S(1)} %copy-done.5, bf16[256,256]{1,0:T(8,128)(2,1)S(1)} %copy-done, f32[1,256]{1,0:T(1,128)S(1)} %bitcast.8, bf16[256,256]{1,0:T(8,128)(2,1)S(1)} %copy.14.w_ref, ...), custom_call_target="tpu_custom_call" | custom-call | tf_op jit(solution)/shard_map/pallas_call | solution.py:469
  48.9 0.6 %slice_bitcast_fusion = f32[64,32]{0,1:T(8,128)} fusion(f32[32,128]{1,0:T(8,128)S(1)} %get-tuple-element.8), kind=kLoop, calls=%fused_computation | loop fusion | bytes 16384 | tf_op jit(solution)/shard_map/transpose | solution.py:517
  49.5 0.1 reshape.24
  49.7 0.1 copy.15
  49.8 0.8 %reshape.25 = f32[32,2,128]{2,1,0:T(2,128)} reshape(f32[32,2,2,2,32]{4,3,2,1,0:T(2,128)S(1)} %copy.15) | data formatting | bytes 65536 | tf_op jit(solution)/shard_map/reshape | solution.py:515
  50.5 0.7 %copy.17 = bf16[256,256]{1,0:T(8,128)(2,1)} copy(bf16[256,256]{1,0:T(8,128)(2,1)S(1)} %get-tuple-element.12) | data formatting | bytes 262144
  (1 shorter events, 0.0 us)
Async XLA Ops:
  1.7 0.8 %copy-start.2 = (bf16[64,256]{1,0:T(8,128)(2,1)S(1)}, bf16[64,256]{1,0:T(8,128)(2,1)}, u32[]{:S(2)}) copy-start(bf16[64,256]{1,0:T(8,128)(2,1)} %wout_ref.1) | copy-start | bytes 98308
  1.7 0.8 %copy-start.3 = (f32[256]{0:T(256)S(1)}, f32[256]{0:T(256)}, u32[]{:S(2)}) copy-start(f32[256]{0:T(256)} %param.8) | copy-start | bytes 3076
  1.7 0.7 %copy-start.4 = (s32[3]{0:T(128)S(1)}, s32[3]{0:T(128)}, u32[]{:S(2)}) copy-start(s32[3]{0:T(128)} %lengths_ref.1) | copy-start | bytes 40
  1.7 0.7 %copy-start.5 = (s32[16]{0:T(128)S(1)}, s32[16]{0:T(128)}, u32[]{:S(2)}) copy-start(s32[16]{0:T(128)} %order_ref.1) | copy-start | bytes 196
  1.7 0.9 %copy-start = (bf16[256,256]{1,0:T(8,128)(2,1)S(1)}, bf16[256,256]{1,0:T(8,128)(2,1)}, u32[]{:S(2)}) copy-start(bf16[256,256]{1,0:T(8,128)(2,1)} %tokens_ref.1) | copy-start | bytes 393220
  1.7 1.0 %copy-start.1 = (bf16[256,256]{1,0:T(8,128)(2,1)S(1)}, bf16[256,256]{1,0:T(8,128)(2,1)}, u32[]{:S(2)}) copy-start(bf16[256,256]{1,0:T(8,128)(2,1)} %gout_ref.1) | copy-start | bytes 393220

commit v3 on v2

--- a/solution.py
+++ b/solution.py
@@ -61,8 +61,8 @@
         )
         return c
 
-    lax.fori_loop(1, n, greet_ctx, 0)
-    lax.fori_loop(1, m, greet_head, 0)
+    lax.fori_loop(1, n, greet_ctx, 0, unroll=keep)
+    lax.fori_loop(1, m, greet_head, 0, unroll=keep)
 
     def ctx_copy(kind, src, dst, slot, sem, peer):
         return pltpu.make_async_remote_copy(
@@ -90,7 +90,7 @@
             copy(kind, src, dst, peer if scatter else mine, mine, peer).start()
             return c
 
-        lax.fori_loop(1, count, step, 0)
+        lax.fori_loop(1, count, step, 0, unroll=keep)
 
     def arrived(copy, kind, src, dst, mine, count, scatter, s):
         origin = lax.rem(mine + count - s, count)
@@ -123,7 +123,7 @@
             return c
 
         hop(kind, buf, me, pair, pair).start()
-        lax.fori_loop(1, lines, step, 0)
+        lax.fori_loop(1, lines, step, 0, unroll=keep)
 
     def relay(kind, buf, s):
         origin = line_origin(s)
@@ -140,7 +140,7 @@
             copy(kind, src, dst, peer if scatter else mine, mine, peer).wait_send()
             return c
 
-        lax.fori_loop(1, count, step, 0)
+        lax.fori_loop(1, count, step, 0, unroll=keep)
 
     x = tokens_ref[...].astype(F32)
     centered = x - jnp.mean(x, axis=1, keepdims=True)
@@ -227,23 +227,42 @@
                 dq_ref[p, h] = slope
             acc_ref[h] += dot_nn(weights, kv)
 
-    def forward_step(s, c):
-        @pl.when(s < lines)
-        def _():
-            @pl.when(s > 0)
-            def _():
-                relay(0, kv_all, s)
-
-            forward(line_origin(s))
-
+    lane_half = lax.broadcasted_iota(jnp.int32, (1, LANES), 1)
+    k_heads = [masked(rolled_b, picks_low), masked(act_b, picks_high)]
+    v_heads = [masked(act_b, picks_low), masked(rolled_b, picks_high)]
+
+    def key_parts(p, part_no):
+        ev_i = order_ref[2 * p + part_no] * block + lane_half
+        live = (evq_ref[:, :LANES] <= ev_i) & (evq_ref[:, :LANES] >= starts(ev_i))
+        scale = jnp.where(live, score_scale, 0.0)
+        q = q_all[p]
+        return [silu_parts(dot_nt(k_heads[part_no][h], q), scale) for h in range(2)]
+
+    def key_prepare(p):
+        if keep:
+            for part_no in range(2):
+                for h, (weights, slope) in enumerate(key_parts(p, part_no)):
+                    wk_ref[p, part_no, h] = weights
+                    dk_ref[p, part_no, h] = slope
+
+    def line_step(s, c):
+        relay(0, kv_all, s)
+        forward(line_origin(s))
+        return c
+
+    def pair_step(s, c):
         @pl.when(s > 0)
         def _():
-            relayed(0, kv_all, s - 1)
-            forward(pair_origin(s - 1))
-
-        return c
-
-    lax.fori_loop(0, lines + 1, forward_step, 0)
+            relay(1, q_all, s)
+
+        key_prepare(line_origin(s))
+        relayed(0, kv_all, s)
+        forward(pair_origin(s))
+        return c
+
+    forward(me)
+    lax.fori_loop(1, lines, line_step, 0, unroll=keep)
+    lax.fori_loop(0, lines, pair_step, 0, unroll=keep)
     attended = jnp.where(low, jnp.where(head0, acc_ref[0], acc_ref[1]), 0.0)
 
     def total(v):
@@ -256,46 +275,19 @@
     st_all[hd] = jnp.transpose(cols)[:8]
     spread(head_copy, 0, st_all, st_all, hd, m, False)
 
-    lane_half = lax.broadcasted_iota(jnp.int32, (1, LANES), 1)
-    ev_k = evq_ref[:, :LANES]
-    k_heads = [masked(rolled_b, picks_low), masked(act_b, picks_high)]
-    v_heads = [masked(act_b, picks_low), masked(rolled_b, picks_high)]
-
-    def key_parts(p, part_no):
-        ev_i = order_ref[2 * p + part_no] * block + lane_half
-        live = (evq_ref[:, :LANES] <= ev_i) & (evq_ref[:, :LANES] >= starts(ev_i))
-        scale = jnp.where(live, score_scale, 0.0)
-        q = q_all[p]
-        return [silu_parts(dot_nt(k_heads[part_no][h], q), scale) for h in range(2)]
-
-    def key_prepare(p):
-        if keep:
-            for part_no in range(2):
-                for h, (weights, slope) in enumerate(key_parts(p, part_no)):
-                    wk_ref[p, part_no, h] = weights
-                    dk_ref[p, part_no, h] = slope
-
-    def relay_queries(s, c):
-        relay(1, q_all, s)
-        return c
-
-    def prepare_line(s, c):
-        key_prepare(line_origin(s))
-        return c
-
     def prepare_pair(s, c):
         relayed(1, q_all, s)
         key_prepare(pair_origin(s))
         return c
 
-    lax.fori_loop(1, lines, relay_queries, 0)
-    lax.fori_loop(0, lines, prepare_line, 0)
+    early = lines // 2
+    lax.fori_loop(0, early, prepare_pair, 0, unroll=keep)
 
     def stats_in(s, c):
         arrived(head_copy, 0, st_all, st_all, hd, m, False, s)
         return c
 
-    lax.fori_loop(1, m, stats_in, 0)
+    lax.fori_loop(1, m, stats_in, 0, unroll=keep)
     stats = st_all[0]
     for i in range(1, m):
         stats = stats + st_all[i]
@@ -323,29 +315,31 @@
 
     attn_grad = attn_grad.astype(BF16)
     ag_heads = masked(attn_grad, picks_low)
-    lax.fori_loop(0, lines, prepare_pair, 0)
+    lax.fori_loop(early, lines, prepare_pair, 0, unroll=keep)
 
     def relay_grads(s, c):
         relay(2, ag_all, s)
         return c
 
-    lax.fori_loop(1, lines, relay_grads, 0)
+    lax.fori_loop(1, lines, relay_grads, 0, unroll=keep)
     acc_ref[...] = jnp.zeros_like(acc_ref)
 
-    def query_back(p, c):
-        kv = kv_all[p]
-        if not keep:
-            scale = query_live(p)
+    def query_back(i, c):
+        kv = kv_all[pl.ds(2 * i, 2)].reshape(2 * rows, LANES)
         for h in range(2):
-            if keep:
-                slope = dq_ref[p, h]
-            else:
-                _, slope = silu_parts(dot_nt(q_heads[h], kv), scale)
-            score_grad = (dot_nt(ag_heads[h], kv) * slope).astype(BF16)
-            acc_ref[h] += dot_nn(score_grad, kv)
-        return c
-
-    lax.fori_loop(0, n, query_back, 0)
+            raw = dot_nt(ag_heads[h], kv)
+            grads = []
+            for b in range(2):
+                if keep:
+                    slope = dq_ref[2 * i + b, h]
+                else:
+                    block_kv = kv[b * rows : (b + 1) * rows]
+                    _, slope = silu_parts(dot_nt(q_heads[h], block_kv), query_live(2 * i + b))
+                grads.append((raw[:, b * rows : (b + 1) * rows] * slope).astype(BF16))
+            acc_ref[h] += dot_nn(jnp.concatenate(grads, axis=1), kv)
+        return c
+
+    lax.fori_loop(0, lines, query_back, 0, unroll=keep)
     query_grad = jnp.where(head0, acc_ref[0], acc_ref[1])
 
     acck_ref[...] = jnp.zeros_like(acck_ref)
@@ -374,8 +368,8 @@
         key_back(pair_origin(s))
         return c
 
-    lax.fori_loop(0, lines, line_back, 0)
-    lax.fori_loop(0, lines, pair_back, 0)
+    lax.fori_loop(0, lines, line_back, 0, unroll=keep)
+    lax.fori_loop(0, lines, pair_back, 0, unroll=keep)
 
     def fold(acc, part_no):
         return jnp.where(head0, acc[part_no, 0], acc[part_no, 1])
@@ -403,7 +397,7 @@
         origin = arrived(head_copy, 1, ip_send, ip_recv, hd, m, True, s)
         return summed + ip_recv[origin].astype(F32)
 
-    input_grad = lax.fori_loop(1, m, parts_in, ip_send[hd].astype(F32))
+    input_grad = lax.fori_loop(1, m, parts_in, ip_send[hd].astype(F32), unroll=keep)
     mine = pl.ds(pl.multiple_of(hd * part, part), part)
     scaled_grad = input_grad * gain_ref[...]
     my_normed = normed_ref[mine]
@@ -419,21 +413,21 @@
         origin = arrived(ctx_copy, 3, wo_send, wo_recv, me, n, True, s)
         return summed + wo_recv[origin].astype(F32)
 
-    wo_sum = lax.fori_loop(1, n, wo_in, wo_send[me].astype(F32))
+    wo_sum = lax.fori_loop(1, n, wo_in, wo_send[me].astype(F32), unroll=keep)
     wo_ref[...] = wo_sum[:chunk]
 
     def uv_in(s, summed):
         origin = arrived(ctx_copy, 4, uv_send, uv_recv, me, n, True, s)
         return summed + uv_recv[origin].astype(F32)
 
-    uv_sum = lax.fori_loop(1, n, uv_in, uv_send[me].astype(F32))
+    uv_sum = lax.fori_loop(1, n, uv_in, uv_send[me].astype(F32), unroll=keep)
     uvqk_ref[...] = uv_sum[:chunk]
 
     def tokens_in(s, c):
         arrived(head_copy, 2, tg_all, tg_all, hd, m, False, s)
         return c
 
-    lax.fori_loop(1, m, tokens_in, 0)
+    lax.fori_loop(1, m, tokens_in, 0, unroll=keep)
     for i in range(m):
         tok_ref[i * part : (i + 1) * part] = tg_all[i]
 

time: 51.3 us -> 47.7 us (0.930)
  Pallas kernels: 46.2 us -> 42.6 us
    pallas_call x1, Pallas kernels: 46.2 us -> 42.6 us  [body(): pl.pallas_call(functools.partial(kernel, n, m, block, lengths.shape[0], 1...]
where the time goes in v3:
time: 47.7 us; the launch traced here: 47.6 us
  Pallas kernels  42.6 us (89%)
  local copies, waits for them, and re-layouts  4.24 us (9%)
  between operations  0.73 us (2%)
    pallas_call x1, Pallas kernels, body(): pl.pallas_call(functools.partial(kernel, n, m, block, lengths.shape[0], 1...  42.6 us
    unnamed x14, local copies, waits for them, and re-layouts  2.54 us

profile of v3, /device:TPU:0, one launch (start us, length us, event | category | flops | bytes accessed | tf_op | source)
XLA Modules:
  0.0 47.6 jit_solution(5577433963527665132)
XLA Ops:
  0.6 1.0 %copy.12 = bf16[256,2,128]{0,2,1:T(8,128)(2,1)S(1)} copy(bf16[256,2,128]{2,1,0:T(2,128)(2,1)} %param.9) | data formatting | bytes 262144 | tf_op args[2]
  1.7 0.0 copy-start.2
  1.7 0.0 copy-start.3
  1.7 0.0 copy-start.4
  1.7 0.0 copy-start.5
  1.7 0.0 copy-start
  1.7 0.0 copy-start.1
  1.7 0.1 copy.14.w_ref
  1.8 0.6 %copy-done.2 = bf16[64,256]{1,0:T(8,128)(2,1)S(1)} copy-done((bf16[64,256]{1,0:T(8,128)(2,1)S(1)}, bf16[64,256]{1,0:T(8,128)(2,1)}, u32[]{:S(2)}) %copy-start.2) | copy-done | bytes 32792
  2.4 0.0 copy-done.3
  2.4 0.0 copy-done.4
  2.4 0.0 copy-done.5
  2.4 0.2 copy-done
  2.6 0.1 copy-done.1
  2.7 42.6 %shard_map.94 = (bf16[256,256]{1,0:T(8,128)(2,1)S(1)}, f32[32,256]{1,0:T(8,128)S(1)}, f32[32,128]{1,0:T(8,128)S(1)}) custom-call(s32[3]{0:T(128)S(1)} %copy-done.4, s32[16]{0:T(128)S(1)} %copy-done.5, bf16[256,256]{1,0:T(8,128)(2,1)S(1)} %copy-done, f32[1,256]{1,0:T(1,128)S(1)} %bitcast.8, bf16[256,256]{1,0:T(8,128)(2,1)S(1)} %copy.14.w_ref, ...), custom_call_target="tpu_custom_call" | custom-call | tf_op jit(solution)/shard_map/pallas_call | solution.py:463
  45.3 0.6 %slice_bitcast_fusion = f32[64,32]{0,1:T(8,128)} fusion(f32[32,128]{1,0:T(8,128)S(1)} %get-tuple-element.8), kind=kLoop, calls=%fused_computation | loop fusion | bytes 16384 | tf_op jit(solution)/shard_map/transpose | solution.py:511
  45.9 0.1 reshape.24
  46.1 0.1 copy.15
  46.1 0.8 %reshape.25 = f32[32,2,128]{2,1,0:T(2,128)} reshape(f32[32,2,2,2,32]{4,3,2,1,0:T(2,128)S(1)} %copy.15) | data formatting | bytes 65536 | tf_op jit(solution)/shard_map/reshape | solution.py:509
  46.9 0.7 %copy.17 = bf16[256,256]{1,0:T(8,128)(2,1)} copy(bf16[256,256]{1,0:T(8,128)(2,1)S(1)} %get-tuple-element.12) | data formatting | bytes 262144
  (1 shorter events, 0.0 us)
Async XLA Ops:
  1.7 0.8 %copy-start.2 = (bf16[64,256]{1,0:T(8,128)(2,1)S(1)}, bf16[64,256]{1,0:T(8,128)(2,1)}, u32[]{:S(2)}) copy-start(bf16[64,256]{1,0:T(8,128)(2,1)} %wout_ref.1) | copy-start | bytes 98308
  1.7 0.8 %copy-start.3 = (f32[256]{0:T(256)S(1)}, f32[256]{0:T(256)}, u32[]{:S(2)}) copy-start(f32[256]{0:T(256)} %param.8) | copy-start | bytes 3076
  1.7 0.7 %copy-start.4 = (s32[3]{0:T(128)S(1)}, s32[3]{0:T(128)}, u32[]{:S(2)}) copy-start(s32[3]{0:T(128)} %lengths_ref.1) | copy-start | bytes 40
  1.7 0.7 %copy-start.5 = (s32[16]{0:T(128)S(1)}, s32[16]{0:T(128)}, u32[]{:S(2)}) copy-start(s32[16]{0:T(128)} %order_ref.1) | copy-start | bytes 196
  1.7 0.9 %copy-start = (bf16[256,256]{1,0:T(8,128)(2,1)S(1)}, bf16[256,256]{1,0:T(8,128)(2,1)}, u32[]{:S(2)}) copy-start(bf16[256,256]{1,0:T(8,128)(2,1)} %tokens_ref.1) | copy-start | bytes 393220
  1.7 1.0 %copy-start.1 = (bf16[256,256]{1,0:T(8,128)(2,1)S(1)}, bf16[256,256]{1,0:T(8,128)(2,1)}, u32[]{:S(2)}) copy-start(bf16[256,256]{1,0:T(8,128)(2,1)} %gout_ref.1) | copy-start | bytes 393220

commit v4 on v3

--- a/solution.py
+++ b/solution.py
@@ -311,7 +311,6 @@
         uv_send[...] = jnp.zeros_like(uv_send)
     for i in range(n):
         wo_send[i, :chunk] = wo_part[i * chunk : (i + 1) * chunk]
-    spread(ctx_copy, 3, wo_send, wo_recv, me, n, True)
 
     attn_grad = attn_grad.astype(BF16)
     ag_heads = masked(attn_grad, picks_low)
@@ -340,6 +339,7 @@
         return c
 
     lax.fori_loop(0, lines, query_back, 0, unroll=keep)
+    spread(ctx_copy, 3, wo_send, wo_recv, me, n, True)
     query_grad = jnp.where(head0, acc_ref[0], acc_ref[1])
 
     acck_ref[...] = jnp.zeros_like(acck_ref)

time: 47.7 us -> 47.7 us (level)
  no operation moved by 1% of the time
where the time goes in v4:
time: 47.7 us; the launch traced here: 47.6 us
  Pallas kernels  42.6 us (89%)
  local copies, waits for them, and re-layouts  4.24 us (9%)
  between operations  0.73 us (2%)
    pallas_call x1, Pallas kernels, body(): pl.pallas_call(functools.partial(kernel, n, m, block, lengths.shape[0], 1...  42.6 us
    unnamed x14, local copies, waits for them, and re-layouts  2.54 us

profile of v4, /device:TPU:0, one launch (start us, length us, event | category | flops | bytes accessed | tf_op | source)
XLA Modules:
  0.0 47.6 jit_solution(9549331746858124956)
XLA Ops:
  0.6 1.0 %copy.12 = bf16[256,2,128]{0,2,1:T(8,128)(2,1)S(1)} copy(bf16[256,2,128]{2,1,0:T(2,128)(2,1)} %param.9) | data formatting | bytes 262144 | tf_op args[2]
  1.7 0.0 copy-start.2
  1.7 0.0 copy-start.3
  1.7 0.0 copy-start.4
  1.7 0.0 copy-start.5
  1.7 0.0 copy-start
  1.7 0.0 copy-start.1
  1.7 0.1 copy.14.w_ref
  1.8 0.6 %copy-done.2 = bf16[64,256]{1,0:T(8,128)(2,1)S(1)} copy-done((bf16[64,256]{1,0:T(8,128)(2,1)S(1)}, bf16[64,256]{1,0:T(8,128)(2,1)}, u32[]{:S(2)}) %copy-start.2) | copy-done | bytes 32792
  2.4 0.0 copy-done.3
  2.4 0.0 copy-done.4
  2.4 0.0 copy-done.5
  2.4 0.2 copy-done
  2.6 0.1 copy-done.1
  2.7 42.6 %shard_map.94 = (bf16[256,256]{1,0:T(8,128)(2,1)S(1)}, f32[32,256]{1,0:T(8,128)S(1)}, f32[32,128]{1,0:T(8,128)S(1)}) custom-call(s32[3]{0:T(128)S(1)} %copy-done.4, s32[16]{0:T(128)S(1)} %copy-done.5, bf16[256,256]{1,0:T(8,128)(2,1)S(1)} %copy-done, f32[1,256]{1,0:T(1,128)S(1)} %bitcast.8, bf16[256,256]{1,0:T(8,128)(2,1)S(1)} %copy.14.w_ref, ...), custom_call_target="tpu_custom_call" | custom-call | tf_op jit(solution)/shard_map/pallas_call | solution.py:463
  45.3 0.6 %slice_bitcast_fusion = f32[64,32]{0,1:T(8,128)} fusion(f32[32,128]{1,0:T(8,128)S(1)} %get-tuple-element.8), kind=kLoop, calls=%fused_computation | loop fusion | bytes 16384 | tf_op jit(solution)/shard_map/transpose | solution.py:511
  45.9 0.1 reshape.24
  46.1 0.1 copy.15
  46.1 0.8 %reshape.25 = f32[32,2,128]{2,1,0:T(2,128)} reshape(f32[32,2,2,2,32]{4,3,2,1,0:T(2,128)S(1)} %copy.15) | data formatting | bytes 65536 | tf_op jit(solution)/shard_map/reshape | solution.py:509
  46.9 0.7 %copy.17 = bf16[256,256]{1,0:T(8,128)(2,1)} copy(bf16[256,256]{1,0:T(8,128)(2,1)S(1)} %get-tuple-element.12) | data formatting | bytes 262144
  (1 shorter events, 0.0 us)
Async XLA Ops:
  1.7 0.8 %copy-start.2 = (bf16[64,256]{1,0:T(8,128)(2,1)S(1)}, bf16[64,256]{1,0:T(8,128)(2,1)}, u32[]{:S(2)}) copy-start(bf16[64,256]{1,0:T(8,128)(2,1)} %wout_ref.1) | copy-start | bytes 98308
  1.7 0.8 %copy-start.3 = (f32[256]{0:T(256)S(1)}, f32[256]{0:T(256)}, u32[]{:S(2)}) copy-start(f32[256]{0:T(256)} %param.8) | copy-start | bytes 3076
  1.7 0.7 %copy-start.4 = (s32[3]{0:T(128)S(1)}, s32[3]{0:T(128)}, u32[]{:S(2)}) copy-start(s32[3]{0:T(128)} %lengths_ref.1) | copy-start | bytes 40
  1.7 0.7 %copy-start.5 = (s32[16]{0:T(128)S(1)}, s32[16]{0:T(128)}, u32[]{:S(2)}) copy-start(s32[16]{0:T(128)} %order_ref.1) | copy-start | bytes 196
  1.7 0.9 %copy-start = (bf16[256,256]{1,0:T(8,128)(2,1)S(1)}, bf16[256,256]{1,0:T(8,128)(2,1)}, u32[]{:S(2)}) copy-start(bf16[256,256]{1,0:T(8,128)(2,1)} %tokens_ref.1) | copy-start | bytes 393220
  1.7 1.0 %copy-start.1 = (bf16[256,256]{1,0:T(8,128)(2,1)S(1)}, bf16[256,256]{1,0:T(8,128)(2,1)}, u32[]{:S(2)}) copy-start(bf16[256,256]{1,0:T(8,128)(2,1)} %gout_ref.1) | copy-start | bytes 393220
